TPU v7x, 32 devices: a whole 2x2x4 slice. The times are simulated.
32 devices in a mesh: groups: 2 (over x), wide: 8 (over z, y), narrow: 2 (over core).
Axes of the slice: x: 2, y: 2, z: 4, core: 2. Of those that a mesh axis runs over, the one named last changes fastest.
Arguments:
- activations: bfloat16 [1024, 9216], P('groups', ('narrow', 'wide')), parts along dimension 0, may hold values from -6 to 6
- up_weight: bfloat16 [9216, 9216], P('narrow', 'wide'), may hold values from -0.0625 to 0.0625
Outputs:
- hidden_out: bfloat16 [1024, 9216], P('groups', ('wide', 'narrow')), parts along dimension 0
There are 2 independent parts, one for each index of `groups`. A program takes and returns all parts, laid end to end along the dimension named above; an argument that names none is the same for every part. Nothing has to cross between parts.
All inputs are finite; a program needn't handle non-finite values.
Results may differ from a plain program's by a relative error of at most 0.001.
Values may be sent and summed in bfloat16 or wider, within the bound.
A program may use at most 64 MiB of HBM per device.

v0:
```python
import jax
import jax.numpy as jnp
from jax import lax
from jax.sharding import PartitionSpec as P


def per_device(activations, up_weight):
    half_features = lax.all_gather(activations, "wide", axis=1, tiled=True)
    partial_value = jnp.dot(half_features, up_weight, preferred_element_type=jnp.float32)
    own_sums = lax.psum_scatter(partial_value, "narrow", scatter_dimension=1, tiled=True)
    return jax.nn.gelu(own_sums, approximate=False).astype(jnp.bfloat16)


def solution(mesh):
    return jax.shard_map(
        per_device,
        mesh=mesh,
        in_specs=(P("groups", ("narrow", "wide")), P("narrow", "wide")),
        out_specs=P("groups", ("wide", "narrow")),
        check_vma=False,
    )
```

profile of v0, /device:TPU:0, one launch (start us, length us, event | category | flops | bytes accessed | tf_op | source)
XLA Modules:
  0.0 125.9 jit_solution(16852736423849786245)
XLA Ops:
  6.5 0.0 all-gather.2.cloned.1.call-start
  6.5 0.7 all-gather.2.cloned.1.call-update
  7.3 0.0 reduce-scatter.2.cloned.1.call-start
  7.3 84.9 %all-gather.2.cloned.1.call-done = bf16[512,4608]{0,1:T(8,128)(2,1)} async-done(((bf16[512,576]{0,1:T(8,128)(2,1)}), bf16[512,4608]{0,1:T(8,128)(2,1)}) %all-gather.2.cloned.1.call-update) | async-done | bytes 4718608 | tf_op jit(solution)/shard_map/all_gather | solution.py:8
  92.2 14.4 %fusion.10 = f32[512,1152]{0,1:T(8,128)} fusion(bf16[512,4608]{0,1:T(8,128)(2,1)} %all-gather.2.cloned.1.call-done, bf16[4608,1152]{1,0:T(8,128)(2,1)} %param.3), kind=kOutput, calls=%fused_computation.19 | convolution fusion | flops 5435817984 | bytes 17694720 | tf_op jit(solution)/shard_map/dot_general | solution.py:9
  106.5 0.0 reduce-scatter.2.cloned.1.call-update
  106.5 8.2 %reduce-scatter.2.cloned.1.call-done = f32[512,576]{0,1:T(8,128)} async-done(((f32[512,1152]{0,1:T(8,128)}), f32[512,576]{0,1:T(8,128)}) %reduce-scatter.2.cloned.1.call-update) | async-done | bytes 1179664 | tf_op jit(solution)/shard_map/reduce_scatter | solution.py:10
  114.8 4.3 %fusion.2 = bf16[512,576]{0,1:T(8,128)(2,1)} fusion(f32[512,576]{0,1:T(8,128)} %reduce-scatter.2.cloned.1.call-done), kind=kLoop, calls=%fused_computation.3 | loop fusion | flops 19169280 | bytes 1769472 | tf_op jit(solution)/shard_map/convert_element_type | solution.py:11
Async XLA Ops:
  6.5 85.6 %all-gather.2.cloned.1.call-start = ((), (), s32[]{:S(2)}) async-start(), calls=%async_computation.1 | async-start | bytes 5308416 | tf_op jit(solution)/shard_map/all_gather | solution.py:8
  7.3 107.5 %reduce-scatter.2.cloned.1.call-start = ((), (), s32[]{:S(2)}) async-start(), calls=%async_computation.2 | async-start | bytes 3538944 | tf_op jit(solution)/shard_map/reduce_scatter | solution.py:10
Sparse Core Ops, SparseCore 0:
  9.5 82.5 all-gather.1
  106.7 8.0 reduce-scatter.1
where the time goes:
time: 126 us
  waiting for transfers between devices  93.8 us (74%)
  matrix products  14.4 us (11%)
  between operations  13.4 us (11%)
  other arithmetic  4.35 us (3%)
    all_gather x1, waiting for transfers between devices, per_device(): half_features = lax.all_gather(activations, 'wide', axis=1, tiled=True)  84.9 us
    dot_general x1, matrix products, per_device(): jnp.dot(half_features, up_weight, preferred_element_type=jnp.float32)  14.4 us
    reduce_scatter x1, waiting for transfers between devices, per_device(): lax.psum_scatter(partial_value, 'narrow', scatter_dimension=1, tiled=True)  8.22 us
    convert_element_type x1, other arithmetic, per_device(): return jax.nn.gelu(own_sums, approximate=False).astype(jnp.bfloat16)  4.35 us
  transfers between devices with their start and end apart: 2, of which 2 were waited for; matrix products, arithmetic and copies ran while one was open for 0% of the time, Pallas kernels for 0%

commit v1 on v0

v1 whole, which is shorter than its diff:
```python
import functools

import jax
import jax.numpy as jnp
from jax import lax
from jax.experimental import pallas as pl
from jax.experimental.pallas import tpu as pltpu
from jax.sharding import PartitionSpec as P

MESH = pl.DeviceIdType.MESH
Y = 2
CHUNKS = 4
LANES = 128
UP, DOWN, ACROSS = 0, 1, 2


def plain(activations, up_weight):
    half_features = lax.all_gather(activations, "wide", axis=1, tiled=True)
    partial_value = jnp.dot(half_features, up_weight, preferred_element_type=jnp.float32)
    own_sums = lax.psum_scatter(partial_value, "narrow", scatter_dimension=1, tiled=True)
    return jax.nn.gelu(own_sums, approximate=False).astype(jnp.bfloat16)


def kernel(
    n_wide, x_ref, w_ref, out_ref,
    buf, wv, w_rem, acc, other,
    w_sem, send_a, send_b, recv_a, recv_b, swap_send, swap_recv,
):
    rows_total, cols = x_ref.shape
    Z = n_wide // Y
    rows = rows_total // CHUNKS
    half = rows // 2
    main = cols // LANES * LANES
    rem = cols - main
    width = 2 * cols
    keep = other.shape[2]

    group = lax.axis_index("groups")
    me = lax.axis_index("wide")
    core = lax.axis_index("narrow")
    z, y = me // Y, me % Y

    def at(zz, yy):
        return zz * Y + yy

    targets = {
        UP: (group, me + Y, core),
        DOWN: (group, me - Y, core),
        ACROSS: (group, at(z, 1 - y), core),
    }
    partner = (group, me, 1 - core)

    w_copy = pltpu.make_async_copy(w_ref, wv, w_sem)
    w_copy.start()

    barrier = pltpu.get_barrier_semaphore()
    for peer in (targets[ACROSS], partner):
        pl.semaphore_signal(barrier, inc=1, device_id=peer, device_id_type=MESH)

    @pl.when(z < Z - 1)
    def _():
        pl.semaphore_signal(barrier, inc=1, device_id=targets[UP], device_id_type=MESH)

    @pl.when(z > 0)
    def _():
        pl.semaphore_signal(barrier, inc=1, device_id=targets[DOWN], device_id_type=MESH)

    for c in range(CHUNKS):
        top = x_ref[c * rows : c * rows + half, :]
        low = x_ref[c * rows + half : (c + 1) * rows, :]
        at_rows = pl.ds(c * half, half)
        buf[me, at_rows, 0:main] = top[:, :main]
        buf[me, at_rows, main : 2 * main] = low[:, :main]
        buf[me, at_rows, 2 * main : width] = jnp.concatenate([top[:, main:], low[:, main:]], axis=1)

    pl.semaphore_wait(barrier, 2 + (z < Z - 1).astype(jnp.int32) + (z > 0).astype(jnp.int32))

    def split(c):
        return width - LANES * (1 + c % 2)

    def copy(kind, c, src, way):
        at_rows = pl.ds(c * half, half)
        if kind == "a":
            ref = buf.at[src, at_rows, 0 : split(c)]
            sends, recvs = send_a, recv_a
        else:
            ref = buf.at[src, at_rows, split(c) : width]
            sends, recvs = send_b, recv_b
        return pltpu.make_async_remote_copy(
            src_ref=ref,
            dst_ref=ref,
            send_sem=sends.at[c, way, src],
            recv_sem=recvs.at[c, src],
            device_id=targets[way],
            device_id_type=MESH,
        )

    def along(kind, c, src, way):
        @pl.when((z < Z - 1) if way == UP else (z > 0))
        def _():
            copy(kind, c, src, way).start()

    def send_own(c):
        along("a", c, me, UP)
        along("a", c, me, DOWN)
        copy("b", c, me, ACROSS).start()
        copy("a", c, me, ACROSS).start()
        along("b", c, me, UP)
        along("b", c, me, DOWN)

    def arrivals(c, d):
        for way, zs in ((UP, z - d), (DOWN, z + d)):
            @pl.when((zs >= 0) & (zs < Z))
            def _():
                src = at(zs, y)
                copy("a", c, src, way).wait_recv()
                along("a", c, src, way)
                copy("a", c, src, ACROSS).start()

        if d == 1:
            src = at(z, 1 - y)
            copy("b", c, src, ACROSS).wait_recv()
            along("b", c, src, UP)
            along("b", c, src, DOWN)
        for way, zs in ((UP, z - d), (DOWN, z + d)):
            @pl.when((zs >= 0) & (zs < Z))
            def _():
                for yy in range(Y):
                    src = at(zs, yy)
                    copy("b", c, src, way).wait_recv()
                    along("b", c, src, way)

    def wait_across(c):
        for zs in range(Z):
            copy("a", c, at(zs, 1 - y), ACROSS).wait_recv()

    def dot(a, b):
        return jnp.dot(a, b, preferred_element_type=jnp.float32)

    def remainders(c):
        at_rows = pl.ds(c * half, half)
        pieces = [buf[w, at_rows, 2 * main : width] for w in range(n_wide)]
        top = jnp.concatenate([p[:, :rem] for p in pieces], axis=1)
        low = jnp.concatenate([p[:, rem:] for p in pieces], axis=1)
        acc[c] = dot(jnp.concatenate([top, low], axis=0), w_rem[...])

    def mains(c, first, last):
        at_rows = pl.ds(c * half, half)

        def step(w, carry):
            lhs = jnp.concatenate(
                [buf[w, at_rows, 0:main], buf[w, at_rows, main : 2 * main]], axis=0
            )
            acc[c] += dot(lhs, wv[pl.ds(pl.multiple_of(w * cols, 64), main), :])
            return carry

        lax.fori_loop(first, last, step, 0)

    def swap(c):
        start = pl.multiple_of((1 - core) * (acc.shape[2] - keep), LANES)
        return pltpu.make_async_remote_copy(
            src_ref=acc.at[c, :, pl.ds(start, keep)],
            dst_ref=other.at[c],
            send_sem=swap_send.at[c],
            recv_sem=swap_recv.at[c],
            device_id=partner,
            device_id_type=MESH,
        )

    def finish(c):
        swap(c).wait_recv()
        start = pl.multiple_of(core * (acc.shape[2] - keep), LANES)
        v = acc[c, :, pl.ds(start, keep)] + other[c]
        hidden = v * (1.0 + lax.erf(v * 0.7071067811865476)) * 0.5
        n = out_ref.shape[1]
        mine = jnp.where(core == 0, hidden[:, :n], hidden[:, keep - n :])
        out_ref[c * rows : (c + 1) * rows, :] = mine.astype(out_ref.dtype)

    send_own(0)
    send_own(1)
    w_copy.wait()
    for w in range(n_wide):
        w_rem[w * rem : (w + 1) * rem, :] = wv[w * cols + main : (w + 1) * cols, :]

    parts = [(0, 3), (3, 6), (6, n_wide)]
    for c in range(CHUNKS):
        if 1 <= c < CHUNKS - 1:
            send_own(c + 1)
        for d in range(1, Z):
            arrivals(c, d)
            if c > 0:
                if d == 1:
                    wait_across(c - 1)
                    remainders(c - 1)
                mains(c - 1, *parts[d - 1])
        if c > 0:
            swap(c - 1).start()
        if c > 1:
            finish(c - 2)
    last = CHUNKS - 1
    wait_across(last)
    remainders(last)
    mains(last, 0, n_wide)
    swap(last).start()
    finish(last - 1)
    finish(last)

    for c in range(CHUNKS):
        swap(c).wait_send()
        copy("b", c, me, ACROSS).wait_send()
        for zs in range(Z):
            copy("a", c, at(zs, y), ACROSS).wait_send()

            @pl.when((zs <= z) & (z < Z - 1))
            def _():
                copy("a", c, at(zs, y), UP).wait_send()
                for yy in range(Y):
                    copy("b", c, at(zs, yy), UP).wait_send()

            @pl.when((zs >= z) & (z > 0))
            def _():
                copy("a", c, at(zs, y), DOWN).wait_send()
                for yy in range(Y):
                    copy("b", c, at(zs, yy), DOWN).wait_send()


def fused(n_wide, activations, up_weight):
    rows, cols = activations.shape
    depth, units = up_weight.shape
    rem = cols % LANES
    keep = (units // 2 + LANES - 1) // LANES * LANES
    return pl.pallas_call(
        functools.partial(kernel, n_wide),
        out_shape=jax.ShapeDtypeStruct((rows, units // 2), jnp.bfloat16),
        in_specs=[
            pl.BlockSpec(memory_space=pltpu.VMEM),
            pl.BlockSpec(memory_space=pl.ANY),
        ],
        out_specs=pl.BlockSpec(memory_space=pltpu.VMEM),
        scratch_shapes=[
            pltpu.VMEM((n_wide, rows // 2, 2 * cols), jnp.bfloat16),
            pltpu.VMEM((depth, units), jnp.bfloat16),
            pltpu.VMEM((n_wide * rem, units), jnp.bfloat16),
            pltpu.VMEM((CHUNKS, rows // CHUNKS, units), jnp.float32),
            pltpu.VMEM((CHUNKS, rows // CHUNKS, keep), jnp.float32),
            pltpu.SemaphoreType.DMA,
            pltpu.SemaphoreType.DMA((CHUNKS, 3, n_wide)),
            pltpu.SemaphoreType.DMA((CHUNKS, 3, n_wide)),
            pltpu.SemaphoreType.DMA((CHUNKS, n_wide)),
            pltpu.SemaphoreType.DMA((CHUNKS, n_wide)),
            pltpu.SemaphoreType.DMA((CHUNKS,)),
            pltpu.SemaphoreType.DMA((CHUNKS,)),
        ],
        compiler_params=pltpu.CompilerParams(
            collective_id=0, has_side_effects=True, vmem_limit_bytes=48 * 2**20
        ),
        cost_estimate=pl.CostEstimate(
            flops=2 * rows * depth * units,
            bytes_accessed=2 * depth * units,
            transcendentals=rows * units // 2,
        ),
    )(activations, up_weight)


def solution(mesh):
    n_wide = mesh.shape["wide"]
    body = functools.partial(fused, n_wide) if n_wide == 4 * Y else plain
    return jax.shard_map(
        body,
        mesh=mesh,
        in_specs=(P("groups", ("narrow", "wide")), P("narrow", "wide")),
        out_specs=P("groups", ("wide", "narrow")),
        check_vma=False,
    )
```

time: 126 us -> 67.9 us (0.54)
  waiting for transfers between devices: 93.8 us -> 0 us
  Pallas kernels: 0 us -> 65.1 us
  matrix products: 14.4 us -> 0 us
  between operations: 13.4 us -> 0.01 us
  other arithmetic: 4.35 us -> 0 us
  local copies, waits for them, and re-layouts: 0 us -> 2.41 us
    all_gather x1 -> x0, waiting for transfers between devices: 84.9 us -> none  [per_device(): half_features = lax.all_gather(activations, 'wide', axis=1, tiled=True)]
    pallas_call x0 -> x1, Pallas kernels: none -> 65.1 us  [fused(): pl.pallas_call(functools.partial(kernel, n_wide), out_shape=jax.ShapeDtyp...]
    dot_general x1 -> x0, matrix products: 14.4 us -> none  [per_device(): jnp.dot(half_features, up_weight, preferred_element_type=jnp.float32)]
    reduce_scatter x1 -> x0, waiting for transfers between devices: 8.22 us -> none  [per_device(): lax.psum_scatter(partial_value, 'narrow', scatter_dimension=1, tiled=True)]
    convert_element_type x1 -> x0, other arithmetic: 4.35 us -> none  [per_device(): return jax.nn.gelu(own_sums, approximate=False).astype(jnp.bfloat16)]
    unnamed x0 -> x1, local copies, waits for them, and re-layouts: none -> 1.36 us
  transfers between devices with their start and end apart: 2 -> 0, of which waited for: 2 -> 0; matrix products, arithmetic and copies ran while one was open for 0% -> 0% of each run, Pallas kernels for 0% -> 0%
where the time goes in v1:
time: 67.9 us; the launch traced here: 67.5 us
  Pallas kernels  65.1 us (96%)
  local copies, waits for them, and re-layouts  2.41 us (4%)
    pallas_call x1, Pallas kernels, fused(): pl.pallas_call(functools.partial(kernel, n_wide), out_shape=jax.ShapeDtyp...  65.1 us

profile of v1, /device:TPU:0, one launch (start us, length us, event | category | flops | bytes accessed | tf_op | source)
XLA Modules:
  0.0 67.5 jit_solution(2822469881862161199)
XLA Ops:
  0.0 1.4 %copy.3.x_ref = bf16[512,576]{1,0:T(8,128)(2,1)S(1)} copy(bf16[512,576]{0,1:T(8,128)(2,1)} %param.2) | data formatting | bytes 1179648 | tf_op args[0]
  1.4 65.1 %shard_map.28 = bf16[512,576]{1,0:T(8,128)(2,1)S(1)} custom-call(bf16[512,576]{1,0:T(8,128)(2,1)S(1)} %copy.3.x_ref, bf16[4608,1152]{1,0:T(8,128)(2,1)} %w_ref.1), custom_call_target="tpu_custom_call" | custom-call | flops 5435817984 | bytes 10616832 | tf_op jit(solution)/shard_map/pallas_call | solution.py:232
  66.5 1.1 %copy.4 = bf16[512,576]{0,1:T(8,128)(2,1)} copy(bf16[512,576]{1,0:T(8,128)(2,1)S(1)} %shard_map.28) | data formatting | bytes 1179648 | tf_op jit(solution)/shard_map/pallas_call | solution.py:232

commit v2 on v0

v2 whole, which is shorter than its diff:
```python
import functools

import jax
import jax.numpy as jnp
from jax import lax
from jax.experimental import pallas as pl
from jax.experimental.pallas import tpu as pltpu
from jax.sharding import PartitionSpec as P

MESH = pl.DeviceIdType.MESH
Y = 2
GROUPS = (64, 64, 48, 32, 48)
LANES = 128
UP, DOWN, ACROSS = 0, 1, 2


def plain(activations, up_weight):
    half_features = lax.all_gather(activations, "wide", axis=1, tiled=True)
    partial_value = jnp.dot(half_features, up_weight, preferred_element_type=jnp.float32)
    own_sums = lax.psum_scatter(partial_value, "narrow", scatter_dimension=1, tiled=True)
    return jax.nn.gelu(own_sums, approximate=False).astype(jnp.bfloat16)


def kernel(
    n_wide, x_ref, w_ref, out_ref,
    buf, wv, acc, other,
    w_sem, send_sem, recv_sem, swap_send, swap_recv,
):
    rows, cols = x_ref.shape
    Z = n_wide // Y
    pairs = rows // 2
    main = cols // LANES * LANES
    rem = cols - main
    width = 2 * cols
    units = wv.shape[1]
    keep = other.shape[2]
    n_a = len(GROUPS) - 1
    last = n_a
    offsets = [sum(GROUPS[:i]) for i in range(len(GROUPS) + 1)]

    group = lax.axis_index("groups")
    me = lax.axis_index("wide")
    core = lax.axis_index("narrow")
    z, y = me // Y, me % Y
    far = jnp.where(z < Z // 2, Z - 1, 0)

    def at(zz, yy):
        return zz * Y + yy

    targets = {
        UP: (group, me + Y, core),
        DOWN: (group, me - Y, core),
        ACROSS: (group, at(z, 1 - y), core),
    }
    partner = (group, me, 1 - core)

    w_copy = pltpu.make_async_copy(w_ref, wv, w_sem)
    w_copy.start()

    barrier = pltpu.get_barrier_semaphore()
    for peer in (targets[ACROSS], partner):
        pl.semaphore_signal(barrier, inc=1, device_id=peer, device_id_type=MESH)

    @pl.when(z < Z - 1)
    def _():
        pl.semaphore_signal(barrier, inc=1, device_id=targets[UP], device_id_type=MESH)

    @pl.when(z > 0)
    def _():
        pl.semaphore_signal(barrier, inc=1, device_id=targets[DOWN], device_id_type=MESH)

    top = x_ref[:pairs, :]
    low = x_ref[pairs:, :]
    buf[me, :, 0:main] = top[:, :main]
    buf[me, :, main : 2 * main] = low[:, :main]
    buf[me, :, 2 * main : width] = jnp.concatenate([top[:, main:], low[:, main:]], axis=1)

    pl.semaphore_wait(barrier, 2 + (z < Z - 1).astype(jnp.int32) + (z > 0).astype(jnp.int32))

    def copy(c, src, way):
        ref = buf.at[src, pl.ds(offsets[c], GROUPS[c]), :]
        return pltpu.make_async_remote_copy(
            src_ref=ref,
            dst_ref=ref,
            send_sem=send_sem.at[c, way, src],
            recv_sem=recv_sem.at[c, src],
            device_id=targets[way],
            device_id_type=MESH,
        )

    def along(c, src, way):
        @pl.when((z < Z - 1) if way == UP else (z > 0))
        def _():
            copy(c, src, way).start()

    def stops(d):
        return (UP, z - d), (DOWN, z + d)

    def pass_on(c, d):
        for way, zs in stops(d):
            @pl.when((zs >= 0) & (zs < Z))
            def _():
                for yy in range(Y) if c == last else (y,):
                    src = at(zs, yy)
                    copy(c, src, way).wait_recv()
                    along(c, src, way)
                    if c != last:
                        copy(c, src, ACROSS).start()

    def wait_across(zs):
        for c in range(n_a):
            copy(c, at(zs, 1 - y), ACROSS).wait_recv()

    def add(src, first, n, fresh=False):
        block = buf[src, pl.ds(first, n), :]
        left = jnp.concatenate([block[:, :main], block[:, 2 * main : 2 * main + rem]], axis=1)
        right = jnp.concatenate([block[:, main : 2 * main], block[:, 2 * main + rem :]], axis=1)
        value = jnp.dot(
            jnp.concatenate([left, right], axis=0),
            wv[pl.ds(pl.multiple_of(src * cols, 64), cols), :],
            preferred_element_type=jnp.float32,
        ).reshape(2, n, units)
        if fresh:
            acc[:, pl.ds(first, n), :] = value
        else:
            acc[:, pl.ds(first, n), :] += value

    def add_at(d, across):
        def step(i, carry):
            zs = z + d * (2 * i - 1)

            @pl.when((zs >= 0) & (zs < Z) & (zs != far))
            def _():
                if across:
                    wait_across(zs)
                add(at(zs, 1 - y if across else y), 0, pairs)

            return carry

        lax.fori_loop(0, 2, step, 0)

    def swap(c):
        start = pl.multiple_of((1 - core) * (units - keep), LANES)
        at_rows = pl.ds(offsets[c], GROUPS[c])
        return pltpu.make_async_remote_copy(
            src_ref=acc.at[:, at_rows, pl.ds(start, keep)],
            dst_ref=other.at[:, at_rows, :],
            send_sem=swap_send.at[c],
            recv_sem=swap_recv.at[c],
            device_id=partner,
            device_id_type=MESH,
        )

    def finish(c):
        swap(c).wait_recv()
        start = pl.multiple_of(core * (units - keep), LANES)
        at_rows = pl.ds(offsets[c], GROUPS[c])
        v = acc[:, at_rows, pl.ds(start, keep)] + other[:, at_rows, :]
        hidden = v * (1.0 + lax.erf(v * 0.7071067811865476)) * 0.5
        n = out_ref.shape[1]
        mine = jnp.where(core == 0, hidden[:, :, :n], hidden[:, :, keep - n :])
        mine = mine.astype(out_ref.dtype)
        for i in range(2):
            out_ref[pl.ds(i * pairs + offsets[c], GROUPS[c]), :] = mine[i]

    copy(last, me, ACROSS).start()
    for c in range(n_a):
        along(c, me, UP)
        along(c, me, DOWN)
        copy(c, me, ACROSS).start()
    along(last, me, UP)
    along(last, me, DOWN)
    copy(last, at(z, 1 - y), ACROSS).wait_recv()
    along(last, at(z, 1 - y), UP)
    along(last, at(z, 1 - y), DOWN)

    def start_sums():
        w_copy.wait()
        add(me, 0, pairs, fresh=True)

    def peer_sums():
        wait_across(z)
        add(at(z, 1 - y), 0, pairs)

    tasks = {
        (1, 0): start_sums,
        (2, 0): lambda: add_at(1, False),
        (2, 1): peer_sums,
        (3, 0): lambda: add_at(2, False),
        (3, 1): lambda: add_at(1, True),
    }
    for d in range(1, Z):
        for c in range(n_a):
            pass_on(c, d)
            if (d, c) in tasks:
                tasks[d, c]()
        if d < Z - 1:
            pass_on(last, d)

    add_at(2, True)
    add(at(far, y), 0, offsets[last])
    for c in range(n_a):
        copy(c, at(far, 1 - y), ACROSS).wait_recv()
        add(at(far, 1 - y), offsets[c], GROUPS[c])
        swap(c).start()
        if c > 0:
            finish(c - 1)
    pass_on(last, Z - 1)
    for yy in range(Y):
        add(at(far, yy), offsets[last], GROUPS[last])
    swap(last).start()
    finish(last - 1)
    finish(last)

    copy(last, me, ACROSS).wait_send()
    for c in range(len(GROUPS)):
        swap(c).wait_send()
        for zs in range(Z):
            if c != last:
                copy(c, at(zs, y), ACROSS).wait_send()
            for way, sent in ((UP, (zs <= z) & (z < Z - 1)), (DOWN, (zs >= z) & (z > 0))):
                @pl.when(sent)
                def _():
                    for yy in range(Y) if c == last else (y,):
                        copy(c, at(zs, yy), way).wait_send()


def fused(n_wide, activations, up_weight):
    rows, cols = activations.shape
    depth, units = up_weight.shape
    keep = (units // 2 + LANES - 1) // LANES * LANES
    return pl.pallas_call(
        functools.partial(kernel, n_wide),
        out_shape=jax.ShapeDtypeStruct((rows, units // 2), jnp.bfloat16),
        in_specs=[
            pl.BlockSpec(memory_space=pltpu.VMEM),
            pl.BlockSpec(memory_space=pl.ANY),
        ],
        out_specs=pl.BlockSpec(memory_space=pltpu.VMEM),
        scratch_shapes=[
            pltpu.VMEM((n_wide, rows // 2, 2 * cols), jnp.bfloat16),
            pltpu.VMEM((depth, units), jnp.bfloat16),
            pltpu.VMEM((2, rows // 2, units), jnp.float32),
            pltpu.VMEM((2, rows // 2, keep), jnp.float32),
            pltpu.SemaphoreType.DMA,
            pltpu.SemaphoreType.DMA((len(GROUPS), 3, n_wide)),
            pltpu.SemaphoreType.DMA((len(GROUPS), n_wide)),
            pltpu.SemaphoreType.DMA((len(GROUPS),)),
            pltpu.SemaphoreType.DMA((len(GROUPS),)),
        ],
        compiler_params=pltpu.CompilerParams(
            collective_id=0, has_side_effects=True, vmem_limit_bytes=48 * 2**20
        ),
        cost_estimate=pl.CostEstimate(
            flops=2 * rows * depth * units,
            bytes_accessed=2 * depth * units,
            transcendentals=rows * units // 2,
        ),
    )(activations, up_weight)


def solution(mesh):
    n_wide = mesh.shape["wide"]
    body = functools.partial(fused, n_wide) if n_wide == 4 * Y else plain
    return jax.shard_map(
        body,
        mesh=mesh,
        in_specs=(P("groups", ("narrow", "wide")), P("narrow", "wide")),
        out_specs=P("groups", ("wide", "narrow")),
        check_vma=False,
    )
```

time: 126 us -> 58.6 us (0.47)
  waiting for transfers between devices: 93.8 us -> 0 us
  Pallas kernels: 0 us -> 55.9 us
  matrix products: 14.4 us -> 0 us
  between operations: 13.4 us -> 0.01 us
  other arithmetic: 4.35 us -> 0 us
  local copies, waits for them, and re-layouts: 0 us -> 2.41 us
    all_gather x1 -> x0, waiting for transfers between devices: 84.9 us -> none  [per_device(): half_features = lax.all_gather(activations, 'wide', axis=1, tiled=True)]
    pallas_call x0 -> x1, Pallas kernels: none -> 55.9 us  [fused(): pl.pallas_call(functools.partial(kernel, n_wide), out_shape=jax.ShapeDtyp...]
    dot_general x1 -> x0, matrix products: 14.4 us -> none  [per_device(): jnp.dot(half_features, up_weight, preferred_element_type=jnp.float32)]
    reduce_scatter x1 -> x0, waiting for transfers between devices: 8.22 us -> none  [per_device(): lax.psum_scatter(partial_value, 'narrow', scatter_dimension=1, tiled=True)]
    convert_element_type x1 -> x0, other arithmetic: 4.35 us -> none  [per_device(): return jax.nn.gelu(own_sums, approximate=False).astype(jnp.bfloat16)]
    unnamed x0 -> x1, local copies, waits for them, and re-layouts: none -> 1.36 us
  transfers between devices with their start and end apart: 2 -> 0, of which waited for: 2 -> 0; matrix products, arithmetic and copies ran while one was open for 0% -> 0% of each run, Pallas kernels for 0% -> 0%
where the time goes in v2:
time: 58.6 us; the launch traced here: 58.3 us
  Pallas kernels  55.9 us (95%)
  local copies, waits for them, and re-layouts  2.41 us (4%)
    pallas_call x1, Pallas kernels, fused(): pl.pallas_call(functools.partial(kernel, n_wide), out_shape=jax.ShapeDtyp...  55.9 us
    unnamed x1, local copies, waits for them, and re-layouts  1.36 us

profile of v2, /device:TPU:0, one launch (start us, length us, event | category | flops | bytes accessed | tf_op | source)
XLA Modules:
  0.0 58.3 jit_solution(9809362607819141794)
XLA Ops:
  0.0 1.4 %copy.3.x_ref = bf16[512,576]{1,0:T(8,128)(2,1)S(1)} copy(bf16[512,576]{0,1:T(8,128)(2,1)} %param.2) | data formatting | bytes 1179648 | tf_op args[0]
  1.4 55.9 %shard_map.28 = bf16[512,576]{1,0:T(8,128)(2,1)S(1)} custom-call(bf16[512,576]{1,0:T(8,128)(2,1)S(1)} %copy.3.x_ref, bf16[4608,1152]{1,0:T(8,128)(2,1)} %w_ref.1), custom_call_target="tpu_custom_call" | custom-call | flops 5435817984 | bytes 10616832 | tf_op jit(solution)/shard_map/pallas_call | solution.py:232
  57.2 1.1 %copy.4 = bf16[512,576]{0,1:T(8,128)(2,1)} copy(bf16[512,576]{1,0:T(8,128)(2,1)S(1)} %shard_map.28) | data formatting | bytes 1179648 | tf_op jit(solution)/shard_map/pallas_call | solution.py:232

commit v3 on v2

--- a/solution.py
+++ b/solution.py
@@ -9,7 +9,7 @@
 
 MESH = pl.DeviceIdType.MESH
 Y = 2
-GROUPS = (64, 64, 48, 32, 48)
+GROUPS = (64, 64, 64, 32, 32)
 LANES = 128
 UP, DOWN, ACROSS = 0, 1, 2
 
@@ -26,7 +26,7 @@
     buf, wv, acc, other,
     w_sem, send_sem, recv_sem, swap_send, swap_recv,
 ):
-    rows, cols = x_ref.shape
+    cols, rows = x_ref.shape
     Z = n_wide // Y
     pairs = rows // 2
     main = cols // LANES * LANES
@@ -69,8 +69,8 @@
     def _():
         pl.semaphore_signal(barrier, inc=1, device_id=targets[DOWN], device_id_type=MESH)
 
-    top = x_ref[:pairs, :]
-    low = x_ref[pairs:, :]
+    own = x_ref[...].T
+    top, low = own[:pairs], own[pairs:]
     buf[me, :, 0:main] = top[:, :main]
     buf[me, :, main : 2 * main] = low[:, :main]
     buf[me, :, 2 * main : width] = jnp.concatenate([top[:, main:], low[:, main:]], axis=1)
@@ -256,7 +256,7 @@
             bytes_accessed=2 * depth * units,
             transcendentals=rows * units // 2,
         ),
-    )(activations, up_weight)
+    )(activations.T, up_weight)
 
 
 def solution(mesh):

time: 58.6 us -> 57.7 us (0.985)
    unnamed x1 -> x2, local copies, waits for them, and re-layouts: 1.36 us -> 1.06 us
where the time goes in v3:
time: 57.7 us; the launch traced here: 57.5 us
  Pallas kernels  55.4 us (96%)
  local copies, waits for them, and re-layouts  2.12 us (4%)
    pallas_call x1, Pallas kernels, fused(): pl.pallas_call(functools.partial(kernel, n_wide), out_shape=jax.ShapeDtyp...  55.4 us

profile of v3, /device:TPU:0, one launch (start us, length us, event | category | flops | bytes accessed | tf_op | source)
XLA Modules:
  0.0 57.5 jit_solution(4874162460171319468)
XLA Ops:
  0.0 0.0 copy-start
  0.0 1.1 %copy-done = bf16[512,576]{0,1:T(8,128)(2,1)S(1)} copy-done((bf16[512,576]{0,1:T(8,128)(2,1)S(1)}, bf16[512,576]{0,1:T(8,128)(2,1)}, u32[]{:S(2)}) %copy-start) | copy-done | bytes 589848
  1.1 55.4 %shard_map.28 = bf16[512,576]{1,0:T(8,128)(2,1)S(1)} custom-call(bf16[576,512]{1,0:T(8,128)(2,1)S(1)} %bitcast.1, bf16[4608,1152]{1,0:T(8,128)(2,1)} %w_ref.1), custom_call_target="tpu_custom_call" | custom-call | flops 5435817984 | bytes 10616832 | tf_op jit(solution)/shard_map/pallas_call | solution.py:232
  56.5 1.1 %copy.3 = bf16[512,576]{0,1:T(8,128)(2,1)} copy(bf16[512,576]{1,0:T(8,128)(2,1)S(1)} %shard_map.28) | data formatting | bytes 1179648 | tf_op jit(solution)/shard_map/pallas_call | solution.py:232
Async XLA Ops:
  0.0 1.1 %copy-start = (bf16[512,576]{0,1:T(8,128)(2,1)S(1)}, bf16[512,576]{0,1:T(8,128)(2,1)}, u32[]{:S(2)}) copy-start(bf16[512,576]{0,1:T(8,128)(2,1)} %param.2) | copy-start | bytes 1769476

commit v4 on v3

--- a/solution.py
+++ b/solution.py
@@ -199,18 +199,23 @@
 
     add_at(2, True)
     add(at(far, y), 0, offsets[last])
-    for c in range(n_a):
+    def far_piece(c):
         copy(c, at(far, 1 - y), ACROSS).wait_recv()
         add(at(far, 1 - y), offsets[c], GROUPS[c])
         swap(c).start()
+
+    for c in range(n_a - 1):
+        far_piece(c)
         if c > 0:
             finish(c - 1)
     pass_on(last, Z - 1)
     for yy in range(Y):
         add(at(far, yy), offsets[last], GROUPS[last])
     swap(last).start()
-    finish(last - 1)
+    finish(n_a - 2)
     finish(last)
+    far_piece(n_a - 1)
+    finish(n_a - 1)
 
     copy(last, me, ACROSS).wait_send()
     for c in range(len(GROUPS)):

time: 57.7 us -> 58 us (level)
  no operation moved by 1% of the time
where the time goes in v4:
time: 58 us; the launch traced here: 57.8 us
  Pallas kernels  55.7 us (96%)
  local copies, waits for them, and re-layouts  2.12 us (4%)
    pallas_call x1, Pallas kernels, fused(): pl.pallas_call(functools.partial(kernel, n_wide), out_shape=jax.ShapeDtyp...  55.7 us

profile of v4, /device:TPU:0, one launch (start us, length us, event | category | flops | bytes accessed | tf_op | source)
XLA Modules:
  0.0 57.8 jit_solution(5843018088399250525)
XLA Ops:
  0.0 0.0 copy-start
  0.0 1.1 %copy-done = bf16[512,576]{0,1:T(8,128)(2,1)S(1)} copy-done((bf16[512,576]{0,1:T(8,128)(2,1)S(1)}, bf16[512,576]{0,1:T(8,128)(2,1)}, u32[]{:S(2)}) %copy-start) | copy-done | bytes 589848
  1.1 55.7 %shard_map.28 = bf16[512,576]{1,0:T(8,128)(2,1)S(1)} custom-call(bf16[576,512]{1,0:T(8,128)(2,1)S(1)} %bitcast.1, bf16[4608,1152]{1,0:T(8,128)(2,1)} %w_ref.1), custom_call_target="tpu_custom_call" | custom-call | flops 5435817984 | bytes 10616832 | tf_op jit(solution)/shard_map/pallas_call | solution.py:237
  56.7 1.1 %copy.3 = bf16[512,576]{0,1:T(8,128)(2,1)} copy(bf16[512,576]{1,0:T(8,128)(2,1)S(1)} %shard_map.28) | data formatting | bytes 1179648 | tf_op jit(solution)/shard_map/pallas_call | solution.py:237
Async XLA Ops:
  0.0 1.1 %copy-start = (bf16[512,576]{0,1:T(8,128)(2,1)S(1)}, bf16[512,576]{0,1:T(8,128)(2,1)}, u32[]{:S(2)}) copy-start(bf16[512,576]{0,1:T(8,128)(2,1)} %param.2) | copy-start | bytes 1769476
